TPU v7x, 32 devices: a whole 2x2x4 slice. The times are simulated.
32 devices in a mesh: strip: 4 (over x, core), section: 8 (over z, y).
Axes of the slice: x: 2, y: 2, z: 4, core: 2. Of those that a mesh axis runs over, the one named last changes fastest.
Arguments:
- features: bfloat16 [8, 8, 128, 1024], P(None, 'strip'), may hold values from -6 to 6
- tile_list: int32 [8, 4, 16], P(None, 'strip'), may hold values from 0 to 15, as said below
- w_reduce: bfloat16 [8, 1024, 256], P('section'), may hold values from -0.1875 to 0.1875
- bias_reduce: bfloat16 [8, 256], P('section'), may hold values from -3 to 3
- w_spatial: bfloat16 [8, 3, 3, 256, 256], P('section'), may hold values from -0.125 to 0.125
- bias_spatial: bfloat16 [8, 256], P('section'), may hold values from -3 to 3
- w_expand: bfloat16 [8, 256, 1024], P('section'), may hold values from -0.375 to 0.375
- bias_expand: bfloat16 [8, 1024], P('section'), may hold values from -3 to 3
Outputs:
- block_maps: bfloat16 [8, 8, 8, 128, 1024], P('section', None, 'strip')
Inputs may be any that keep to these rules, and one draw needn't show every extreme that they name: `tile_list`: each strip's row lists the tissue tiles of that strip, padded to 16 entries by repeats of its first entry; in each slide window one strip is all tissue.
All inputs are finite; a program needn't handle non-finite values.
Results may differ from a plain program's by a relative error of at most 0.02.
Values may be sent and summed in bfloat16 or wider, within the bound.
A program may use at most 64 MiB of HBM per device.

v0:
```python
import jax
import jax.numpy as jnp
from jax import lax
from jax.sharding import PartitionSpec as P

TILE_W = 8


def extended(cells, sides, width):
    for axis, dim in sides:
        count = lax.axis_size(axis)
        ends = count - 1
        head = lax.slice_in_dim(cells, 0, width, axis=dim)
        tail = lax.slice_in_dim(cells, cells.shape[dim] - width, cells.shape[dim], axis=dim)
        cells = jnp.concatenate(
            [
                lax.ppermute(tail, axis, [(i, (i + 1) % count) for i in range(ends)]),
                cells,
                lax.ppermute(head, axis, [((i + 1) % count, i) for i in range(ends)]),
            ],
            axis=dim,
        )
    return cells


def passed_along(value, axis, steps):
    count = lax.axis_size(axis)
    leading, last = (max(0, -steps), min(count, count - steps))
    return lax.ppermute(value, axis, [(source, source + steps) for source in range(leading, last)])


def tissue_mask(tile_list, rows):
    tiles_count = tile_list.shape[-1]
    columns = jnp.arange(tiles_count, dtype=jnp.int32)
    hits = jnp.any(tile_list[..., :, None] == columns[None, None, None, :], axis=-2)
    tissue = hits.astype(jnp.float32)
    tissue = jnp.repeat(tissue, rows, axis=1)
    return jnp.repeat(tissue, TILE_W, axis=2)


def reduce_part(maps, w_one, b_one):
    slides, rows, cols, chans = maps.shape
    inner = w_one.shape[1]
    reduced = jax.nn.relu(
        jnp.dot(maps.reshape(-1, chans), w_one, preferred_element_type=jnp.float32)
        + b_one.astype(jnp.float32)
    )
    return reduced.astype(jnp.bfloat16).reshape(slides, rows, cols, inner)


def finish_block(maps, padded, tissue, w_two, b_two, w_three, b_three):
    slides, rows, cols, chans = maps.shape
    inner = w_two.shape[-1]
    accumulated = jnp.zeros((slides * rows * cols, inner), jnp.float32)
    for row_off in range(3):
        for col_off in range(3):
            window = padded[:, row_off : row_off + rows, col_off : col_off + cols].reshape(
                -1, inner
            )
            accumulated = accumulated + jnp.dot(
                window, w_two[row_off, col_off], preferred_element_type=jnp.float32
            )
    spatial = jax.nn.relu(accumulated + b_two.astype(jnp.float32)).astype(jnp.bfloat16)
    expanded = jnp.dot(spatial, w_three, preferred_element_type=jnp.float32) + b_three.astype(
        jnp.float32
    )
    flat = maps.reshape(-1, chans).astype(jnp.float32)
    result = jax.nn.relu(flat + expanded) * tissue.reshape(-1, 1)
    return result.astype(jnp.bfloat16).reshape(slides, rows, cols, chans)


def shards(
    features, tile_list, w_reduce, bias_reduce, w_spatial, bias_spatial, w_expand, bias_expand
):
    section_index = lax.axis_index("section")
    section_count = lax.axis_size("section")
    slide_count = features.shape[0]
    rows = features.shape[1]
    tissue = tissue_mask(tile_list, rows)
    step_count = slide_count + section_count - 1

    def one_step(step, state):
        carried, result = state
        pick = jnp.minimum(step, slide_count - 1).astype(jnp.int32)
        first = lax.dynamic_slice_in_dim(features, pick, 1, 0)
        inputs_now = jnp.where(section_index == 0, first, carried)
        offset = step - section_index
        active = jnp.logical_and(offset >= 0, offset < slide_count)
        slide_now = jnp.clip(offset, 0, slide_count - 1)
        tissue_part = lax.dynamic_slice_in_dim(tissue, slide_now, 1, 0)
        reduced = reduce_part(inputs_now, w_reduce[0], bias_reduce[0])
        padded = extended(reduced, (("strip", 1),), 1)
        padded = jnp.pad(padded, ((0, 0), (0, 0), (1, 1), (0, 0)))
        produced = finish_block(
            inputs_now,
            padded,
            tissue_part,
            w_spatial[0],
            bias_spatial[0],
            w_expand[0],
            bias_expand[0],
        )
        current = lax.dynamic_slice_in_dim(result, slide_now, 1, 0)
        result = lax.dynamic_update_slice_in_dim(
            result, jnp.where(active, produced, current), slide_now, 0
        )
        carried = passed_along(produced, "section", 1)
        return (carried, result)

    start_state = (jnp.zeros_like(features[0:1]), jnp.zeros_like(features))
    final_state = lax.fori_loop(0, step_count, one_step, start_state)
    return final_state[1][None]


def solution(mesh):
    in_specs = (
        P(None, "strip", None, None),
        P(None, "strip", None),
        P("section", None, None),
        P("section", None),
        P("section", None, None, None, None),
        P("section", None),
        P("section", None, None),
        P("section", None),
    )
    out_specs = P("section", None, "strip", None, None)
    return jax.shard_map(shards, mesh=mesh, in_specs=in_specs, out_specs=out_specs, check_vma=False)
```

profile of v0, /device:TPU:29, one launch (start us, length us, event | category | flops | bytes accessed | tf_op | source)
XLA Modules:
  0.0 421.6 jit_solution(17953006636013688038)
XLA Ops:
  1.1 2.5 broadcast_in_dim.29
  3.7 418.0 %while.17 = (s32[]{:T(128)}, bf16[1,2,128,1024]{3,2,1,0:T(8,128)(2,1)S(1)}, bf16[8,2,128,1024]{3,2,1,0:T(8,128)(2,1)}, pred[]{:T(512)}, bf16[8,2,128,1024]{3,2,1...) while((s32[]{:T(128)}, ...), condition=%wide.region_2.3_spmd, body=%wide.region_1.2_spmd.sunk | while | flops 575170048 | bytes 17979784 | solution.py:111
  6.2 2.6 collective-permute-start
  8.8 3.0 collective-permute-start.1
  17.8 2.0 select_dynamic-update-slice_fusion.2
  19.8 11.6 %collective-permute-done.2 = bf16[1,2,128,1024]{3,2,1,0:T(8,128)(2,1)S(1)} collective-permute-done((bf16[1,2,128,1024]{3,2,1,0:T(8,128)(2,1)S(1)}, bf16[1,2,128,1024]{3,2,1,0:T(8,128)(2,1)S(1)}, u32[]{:S(2)}, u32[]{:S(2)}) %collective-permute-start.2) | collective-permute-done | bytes 524320 | tf_op jit(solution)/shard_map/while/body/eval_jaxpr/ppermute | solution.py:29
  34.0 2.1 collective-permute-start
  36.1 3.5 collective-permute-start.1
  42.6 1.5 fusion.73
  45.5 2.0 select_dynamic-update-slice_fusion.2
  47.5 11.2 %collective-permute-done.2 = bf16[1,2,128,1024]{3,2,1,0:T(8,128)(2,1)S(1)} collective-permute-done((bf16[1,2,128,1024]{3,2,1,0:T(8,128)(2,1)S(1)}, bf16[1,2,128,1024]{3,2,1,0:T(8,128)(2,1)S(1)}, u32[]{:S(2)}, u32[]{:S(2)}) %collective-permute-start.2) | collective-permute-done | bytes 524320 | tf_op jit(solution)/shard_map/while/body/eval_jaxpr/ppermute | solution.py:29
  61.2 1.9 collective-permute-start
  63.1 3.6 collective-permute-start.1
  69.8 1.5 fusion.73
  72.7 2.0 select_dynamic-update-slice_fusion.2
  74.7 11.3 %collective-permute-done.2 = bf16[1,2,128,1024]{3,2,1,0:T(8,128)(2,1)S(1)} collective-permute-done((bf16[1,2,128,1024]{3,2,1,0:T(8,128)(2,1)S(1)}, bf16[1,2,128,1024]{3,2,1,0:T(8,128)(2,1)S(1)}, u32[]{:S(2)}, u32[]{:S(2)}) %collective-permute-start.2) | collective-permute-done | bytes 524320 | tf_op jit(solution)/shard_map/while/body/eval_jaxpr/ppermute | solution.py:29
  88.6 1.9 collective-permute-start
  90.5 3.6 collective-permute-start.1
  100.0 2.0 select_dynamic-update-slice_fusion.2
  102.1 11.9 %collective-permute-done.2 = bf16[1,2,128,1024]{3,2,1,0:T(8,128)(2,1)S(1)} collective-permute-done((bf16[1,2,128,1024]{3,2,1,0:T(8,128)(2,1)S(1)}, bf16[1,2,128,1024]{3,2,1,0:T(8,128)(2,1)S(1)}, u32[]{:S(2)}, u32[]{:S(2)}) %collective-permute-start.2) | collective-permute-done | bytes 524320 | tf_op jit(solution)/shard_map/while/body/eval_jaxpr/ppermute | solution.py:29
  116.5 1.9 collective-permute-start
  118.4 3.6 collective-permute-start.1
  128.0 2.0 select_dynamic-update-slice_fusion.2
  130.1 11.9 %collective-permute-done.2 = bf16[1,2,128,1024]{3,2,1,0:T(8,128)(2,1)S(1)} collective-permute-done((bf16[1,2,128,1024]{3,2,1,0:T(8,128)(2,1)S(1)}, bf16[1,2,128,1024]{3,2,1,0:T(8,128)(2,1)S(1)}, u32[]{:S(2)}, u32[]{:S(2)}) %collective-permute-start.2) | collective-permute-done | bytes 524320 | tf_op jit(solution)/shard_map/while/body/eval_jaxpr/ppermute | solution.py:29
  144.5 1.9 collective-permute-start
  146.4 3.6 collective-permute-start.1
  156.0 2.0 select_dynamic-update-slice_fusion.2
  158.0 11.9 %collective-permute-done.2 = bf16[1,2,128,1024]{3,2,1,0:T(8,128)(2,1)S(1)} collective-permute-done((bf16[1,2,128,1024]{3,2,1,0:T(8,128)(2,1)S(1)}, bf16[1,2,128,1024]{3,2,1,0:T(8,128)(2,1)S(1)}, u32[]{:S(2)}, u32[]{:S(2)}) %collective-permute-start.2) | collective-permute-done | bytes 524320 | tf_op jit(solution)/shard_map/while/body/eval_jaxpr/ppermute | solution.py:29
  172.5 1.9 collective-permute-start
  174.4 3.7 collective-permute-start.1
  184.0 2.0 select_dynamic-update-slice_fusion.2
  186.0 11.9 %collective-permute-done.2 = bf16[1,2,128,1024]{3,2,1,0:T(8,128)(2,1)S(1)} collective-permute-done((bf16[1,2,128,1024]{3,2,1,0:T(8,128)(2,1)S(1)}, bf16[1,2,128,1024]{3,2,1,0:T(8,128)(2,1)S(1)}, u32[]{:S(2)}, u32[]{:S(2)}) %collective-permute-start.2) | collective-permute-done | bytes 524320 | tf_op jit(solution)/shard_map/while/body/eval_jaxpr/ppermute | solution.py:29
  200.4 1.9 collective-permute-start
  202.3 3.8 collective-permute-start.1
  212.0 2.0 select_dynamic-update-slice_fusion.2
  214.1 11.8 %collective-permute-done.2 = bf16[1,2,128,1024]{3,2,1,0:T(8,128)(2,1)S(1)} collective-permute-done((bf16[1,2,128,1024]{3,2,1,0:T(8,128)(2,1)S(1)}, bf16[1,2,128,1024]{3,2,1,0:T(8,128)(2,1)S(1)}, u32[]{:S(2)}, u32[]{:S(2)}) %collective-permute-start.2) | collective-permute-done | bytes 524320 | tf_op jit(solution)/shard_map/while/body/eval_jaxpr/ppermute | solution.py:29
  228.4 1.9 collective-permute-start
  230.3 3.8 collective-permute-start.1
  240.1 2.0 select_dynamic-update-slice_fusion.2
  242.1 11.7 %collective-permute-done.2 = bf16[1,2,128,1024]{3,2,1,0:T(8,128)(2,1)S(1)} collective-permute-done((bf16[1,2,128,1024]{3,2,1,0:T(8,128)(2,1)S(1)}, bf16[1,2,128,1024]{3,2,1,0:T(8,128)(2,1)S(1)}, u32[]{:S(2)}, u32[]{:S(2)}) %collective-permute-start.2) | collective-permute-done | bytes 524320 | tf_op jit(solution)/shard_map/while/body/eval_jaxpr/ppermute | solution.py:29
  256.3 1.9 collective-permute-start
  258.3 3.9 collective-permute-start.1
  268.1 2.0 select_dynamic-update-slice_fusion.2
  270.1 11.7 %collective-permute-done.2 = bf16[1,2,128,1024]{3,2,1,0:T(8,128)(2,1)S(1)} collective-permute-done((bf16[1,2,128,1024]{3,2,1,0:T(8,128)(2,1)S(1)}, bf16[1,2,128,1024]{3,2,1,0:T(8,128)(2,1)S(1)}, u32[]{:S(2)}, u32[]{:S(2)}) %collective-permute-start.2) | collective-permute-done | bytes 524320 | tf_op jit(solution)/shard_map/while/body/eval_jaxpr/ppermute | solution.py:29
  284.3 1.9 collective-permute-start
  286.2 3.9 collective-permute-start.1
  296.1 2.0 select_dynamic-update-slice_fusion.2
  298.2 11.6 %collective-permute-done.2 = bf16[1,2,128,1024]{3,2,1,0:T(8,128)(2,1)S(1)} collective-permute-done((bf16[1,2,128,1024]{3,2,1,0:T(8,128)(2,1)S(1)}, bf16[1,2,128,1024]{3,2,1,0:T(8,128)(2,1)S(1)}, u32[]{:S(2)}, u32[]{:S(2)}) %collective-permute-start.2) | collective-permute-done | bytes 524320 | tf_op jit(solution)/shard_map/while/body/eval_jaxpr/ppermute | solution.py:29
  312.3 1.9 collective-permute-start
  314.2 4.0 collective-permute-start.1
  324.1 2.0 select_dynamic-update-slice_fusion.2
  326.2 11.5 %collective-permute-done.2 = bf16[1,2,128,1024]{3,2,1,0:T(8,128)(2,1)S(1)} collective-permute-done((bf16[1,2,128,1024]{3,2,1,0:T(8,128)(2,1)S(1)}, bf16[1,2,128,1024]{3,2,1,0:T(8,128)(2,1)S(1)}, u32[]{:S(2)}, u32[]{:S(2)}) %collective-permute-start.2) | collective-permute-done | bytes 524320 | tf_op jit(solution)/shard_map/while/body/eval_jaxpr/ppermute | solution.py:29
  340.2 1.9 collective-permute-start
  342.2 4.1 collective-permute-start.1
  352.2 2.0 select_dynamic-update-slice_fusion.2
  354.2 11.5 %collective-permute-done.2 = bf16[1,2,128,1024]{3,2,1,0:T(8,128)(2,1)S(1)} collective-permute-done((bf16[1,2,128,1024]{3,2,1,0:T(8,128)(2,1)S(1)}, bf16[1,2,128,1024]{3,2,1,0:T(8,128)(2,1)S(1)}, u32[]{:S(2)}, u32[]{:S(2)}) %collective-permute-start.2) | collective-permute-done | bytes 524320 | tf_op jit(solution)/shard_map/while/body/eval_jaxpr/ppermute | solution.py:29
  368.2 1.9 collective-permute-start
  370.1 4.1 collective-permute-start.1
  380.2 2.0 select_dynamic-update-slice_fusion.2
  382.2 11.4 %collective-permute-done.2 = bf16[1,2,128,1024]{3,2,1,0:T(8,128)(2,1)S(1)} collective-permute-done((bf16[1,2,128,1024]{3,2,1,0:T(8,128)(2,1)S(1)}, bf16[1,2,128,1024]{3,2,1,0:T(8,128)(2,1)S(1)}, u32[]{:S(2)}, u32[]{:S(2)}) %collective-permute-start.2) | collective-permute-done | bytes 524320 | tf_op jit(solution)/shard_map/while/body/eval_jaxpr/ppermute | solution.py:29
  396.2 1.9 collective-permute-start
  398.1 4.2 collective-permute-start.1
  408.2 2.0 select_dynamic-update-slice_fusion.2
  410.3 11.3 %collective-permute-done.2 = bf16[1,2,128,1024]{3,2,1,0:T(8,128)(2,1)S(1)} collective-permute-done((bf16[1,2,128,1024]{3,2,1,0:T(8,128)(2,1)S(1)}, bf16[1,2,128,1024]{3,2,1,0:T(8,128)(2,1)S(1)}, u32[]{:S(2)}, u32[]{:S(2)}) %collective-permute-start.2) | collective-permute-done | bytes 524320 | tf_op jit(solution)/shard_map/while/body/eval_jaxpr/ppermute | solution.py:29
  (342 shorter events, 122.4 us)
Async XLA Ops:
  1.1 2.6 copy-start
  1.1 2.6 copy-start.1
  1.1 2.6 copy-start.2
  1.1 2.6 copy-start.3
  6.2 5.7 %collective-permute-start = (bf16[1,1,128,256]{3,2,1,0:T(8,128)(2,1)S(1)}, bf16[1,1,128,256]{3,2,1,0:T(8,128)(2,1)S(1)}, u32[]{:S(2)}, u32[]{:S(2)}) collective-permute-start(bf16[1,1,128,256]{3,2,1,0:T(8,128)(2,1)S(1)} %get-tuple-element.423), channel_id=1, source_target_pairs={{8,0},{16,8},{24,16},{9,1},{17,9},{25,17},{10,2},{18,10},{26,18},{... | collective-permute-start | bytes 196616 | tf_op jit(solution)/shard_map/while/body/eval_jaxpr/ppermute | solution.py:19
  8.8 4.3 %collective-permute-start.1 = (bf16[1,1,128,256]{3,2,1,0:T(8,128)(2,1)S(1)}, bf16[1,1,128,256]{3,2,1,0:T(8,128)(2,1)S(1)}, u32[]{:S(2)}, u32[]{:S(2)}) collective-permute-start(bf16[1,1,128,256]{3,2,1,0:T(8,128)(2,1)S(1)} %get-tuple-element.424), channel_id=1, source_target_pairs={{0,8},{8,16},{16,24},{1,9},{9,17},{17,25},{2,10},{10,18},{18,26},{... | collective-permute-start | bytes 196616 | tf_op jit(solution)/shard_map/while/body/eval_jaxpr/ppermute | solution.py:17
  16.5 15.0 %collective-permute-start.2 = (bf16[1,2,128,1024]{3,2,1,0:T(8,128)(2,1)S(1)}, bf16[1,2,128,1024]{3,2,1,0:T(8,128)(2,1)S(1)}, u32[]{:S(2)}, u32[]{:S(2)}) collective-permute-start(bf16[1,2,128,1024]{3,2,1,0:T(8,128)(2,1)S(1)} %bitcast.157), channel_id=1, source_target_pairs={{0,1},{1,2},{2,3},{3,4},{4,5},{5,6},{6,7},{8,9},{9,10},{10,11},{11... | collective-permute-start | bytes 1572872 | tf_op jit(solution)/shard_map/while/body/eval_jaxpr/ppermute | solution.py:29
  34.0 5.6 %collective-permute-start = (bf16[1,1,128,256]{3,2,1,0:T(8,128)(2,1)S(1)}, bf16[1,1,128,256]{3,2,1,0:T(8,128)(2,1)S(1)}, u32[]{:S(2)}, u32[]{:S(2)}) collective-permute-start(bf16[1,1,128,256]{3,2,1,0:T(8,128)(2,1)S(1)} %get-tuple-element.423), channel_id=1, source_target_pairs={{8,0},{16,8},{24,16},{9,1},{17,9},{25,17},{10,2},{18,10},{26,18},{... | collective-permute-start | bytes 196616 | tf_op jit(solution)/shard_map/while/body/eval_jaxpr/ppermute | solution.py:19
  36.1 4.8 %collective-permute-start.1 = (bf16[1,1,128,256]{3,2,1,0:T(8,128)(2,1)S(1)}, bf16[1,1,128,256]{3,2,1,0:T(8,128)(2,1)S(1)}, u32[]{:S(2)}, u32[]{:S(2)}) collective-permute-start(bf16[1,1,128,256]{3,2,1,0:T(8,128)(2,1)S(1)} %get-tuple-element.424), channel_id=1, source_target_pairs={{0,8},{8,16},{16,24},{1,9},{9,17},{17,25},{2,10},{10,18},{18,26},{... | collective-permute-start | bytes 196616 | tf_op jit(solution)/shard_map/while/body/eval_jaxpr/ppermute | solution.py:17
  44.1 14.5 %collective-permute-start.2 = (bf16[1,2,128,1024]{3,2,1,0:T(8,128)(2,1)S(1)}, bf16[1,2,128,1024]{3,2,1,0:T(8,128)(2,1)S(1)}, u32[]{:S(2)}, u32[]{:S(2)}) collective-permute-start(bf16[1,2,128,1024]{3,2,1,0:T(8,128)(2,1)S(1)} %bitcast.157), channel_id=1, source_target_pairs={{0,1},{1,2},{2,3},{3,4},{4,5},{5,6},{6,7},{8,9},{9,10},{10,11},{11... | collective-permute-start | bytes 1572872 | tf_op jit(solution)/shard_map/while/body/eval_jaxpr/ppermute | solution.py:29
  61.2 5.6 %collective-permute-start = (bf16[1,1,128,256]{3,2,1,0:T(8,128)(2,1)S(1)}, bf16[1,1,128,256]{3,2,1,0:T(8,128)(2,1)S(1)}, u32[]{:S(2)}, u32[]{:S(2)}) collective-permute-start(bf16[1,1,128,256]{3,2,1,0:T(8,128)(2,1)S(1)} %get-tuple-element.423), channel_id=1, source_target_pairs={{8,0},{16,8},{24,16},{9,1},{17,9},{25,17},{10,2},{18,10},{26,18},{... | collective-permute-start | bytes 196616 | tf_op jit(solution)/shard_map/while/body/eval_jaxpr/ppermute | solution.py:19
  63.1 5.0 %collective-permute-start.1 = (bf16[1,1,128,256]{3,2,1,0:T(8,128)(2,1)S(1)}, bf16[1,1,128,256]{3,2,1,0:T(8,128)(2,1)S(1)}, u32[]{:S(2)}, u32[]{:S(2)}) collective-permute-start(bf16[1,1,128,256]{3,2,1,0:T(8,128)(2,1)S(1)} %get-tuple-element.424), channel_id=1, source_target_pairs={{0,8},{8,16},{16,24},{1,9},{9,17},{17,25},{2,10},{10,18},{18,26},{... | collective-permute-start | bytes 196616 | tf_op jit(solution)/shard_map/while/body/eval_jaxpr/ppermute | solution.py:17
  71.4 14.6 %collective-permute-start.2 = (bf16[1,2,128,1024]{3,2,1,0:T(8,128)(2,1)S(1)}, bf16[1,2,128,1024]{3,2,1,0:T(8,128)(2,1)S(1)}, u32[]{:S(2)}, u32[]{:S(2)}) collective-permute-start(bf16[1,2,128,1024]{3,2,1,0:T(8,128)(2,1)S(1)} %bitcast.157), channel_id=1, source_target_pairs={{0,1},{1,2},{2,3},{3,4},{4,5},{5,6},{6,7},{8,9},{9,10},{10,11},{11... | collective-permute-start | bytes 1572872 | tf_op jit(solution)/shard_map/while/body/eval_jaxpr/ppermute | solution.py:29
  88.6 5.6 %collective-permute-start = (bf16[1,1,128,256]{3,2,1,0:T(8,128)(2,1)S(1)}, bf16[1,1,128,256]{3,2,1,0:T(8,128)(2,1)S(1)}, u32[]{:S(2)}, u32[]{:S(2)}) collective-permute-start(bf16[1,1,128,256]{3,2,1,0:T(8,128)(2,1)S(1)} %get-tuple-element.423), channel_id=1, source_target_pairs={{8,0},{16,8},{24,16},{9,1},{17,9},{25,17},{10,2},{18,10},{26,18},{... | collective-permute-start | bytes 196616 | tf_op jit(solution)/shard_map/while/body/eval_jaxpr/ppermute | solution.py:19
  90.5 5.0 %collective-permute-start.1 = (bf16[1,1,128,256]{3,2,1,0:T(8,128)(2,1)S(1)}, bf16[1,1,128,256]{3,2,1,0:T(8,128)(2,1)S(1)}, u32[]{:S(2)}, u32[]{:S(2)}) collective-permute-start(bf16[1,1,128,256]{3,2,1,0:T(8,128)(2,1)S(1)} %get-tuple-element.424), channel_id=1, source_target_pairs={{0,8},{8,16},{16,24},{1,9},{9,17},{17,25},{2,10},{10,18},{18,26},{... | collective-permute-start | bytes 196616 | tf_op jit(solution)/shard_map/while/body/eval_jaxpr/ppermute | solution.py:17
  98.7 15.3 %collective-permute-start.2 = (bf16[1,2,128,1024]{3,2,1,0:T(8,128)(2,1)S(1)}, bf16[1,2,128,1024]{3,2,1,0:T(8,128)(2,1)S(1)}, u32[]{:S(2)}, u32[]{:S(2)}) collective-permute-start(bf16[1,2,128,1024]{3,2,1,0:T(8,128)(2,1)S(1)} %bitcast.157), channel_id=1, source_target_pairs={{0,1},{1,2},{2,3},{3,4},{4,5},{5,6},{6,7},{8,9},{9,10},{10,11},{11... | collective-permute-start | bytes 1572872 | tf_op jit(solution)/shard_map/while/body/eval_jaxpr/ppermute | solution.py:29
  116.5 5.6 %collective-permute-start = (bf16[1,1,128,256]{3,2,1,0:T(8,128)(2,1)S(1)}, bf16[1,1,128,256]{3,2,1,0:T(8,128)(2,1)S(1)}, u32[]{:S(2)}, u32[]{:S(2)}) collective-permute-start(bf16[1,1,128,256]{3,2,1,0:T(8,128)(2,1)S(1)} %get-tuple-element.423), channel_id=1, source_target_pairs={{8,0},{16,8},{24,16},{9,1},{17,9},{25,17},{10,2},{18,10},{26,18},{... | collective-permute-start | bytes 196616 | tf_op jit(solution)/shard_map/while/body/eval_jaxpr/ppermute | solution.py:19
  118.4 5.0 %collective-permute-start.1 = (bf16[1,1,128,256]{3,2,1,0:T(8,128)(2,1)S(1)}, bf16[1,1,128,256]{3,2,1,0:T(8,128)(2,1)S(1)}, u32[]{:S(2)}, u32[]{:S(2)}) collective-permute-start(bf16[1,1,128,256]{3,2,1,0:T(8,128)(2,1)S(1)} %get-tuple-element.424), channel_id=1, source_target_pairs={{0,8},{8,16},{16,24},{1,9},{9,17},{17,25},{2,10},{10,18},{18,26},{... | collective-permute-start | bytes 196616 | tf_op jit(solution)/shard_map/while/body/eval_jaxpr/ppermute | solution.py:17
  126.7 15.2 %collective-permute-start.2 = (bf16[1,2,128,1024]{3,2,1,0:T(8,128)(2,1)S(1)}, bf16[1,2,128,1024]{3,2,1,0:T(8,128)(2,1)S(1)}, u32[]{:S(2)}, u32[]{:S(2)}) collective-permute-start(bf16[1,2,128,1024]{3,2,1,0:T(8,128)(2,1)S(1)} %bitcast.157), channel_id=1, source_target_pairs={{0,1},{1,2},{2,3},{3,4},{4,5},{5,6},{6,7},{8,9},{9,10},{10,11},{11... | collective-permute-start | bytes 1572872 | tf_op jit(solution)/shard_map/while/body/eval_jaxpr/ppermute | solution.py:29
  144.5 5.6 %collective-permute-start = (bf16[1,1,128,256]{3,2,1,0:T(8,128)(2,1)S(1)}, bf16[1,1,128,256]{3,2,1,0:T(8,128)(2,1)S(1)}, u32[]{:S(2)}, u32[]{:S(2)}) collective-permute-start(bf16[1,1,128,256]{3,2,1,0:T(8,128)(2,1)S(1)} %get-tuple-element.423), channel_id=1, source_target_pairs={{8,0},{16,8},{24,16},{9,1},{17,9},{25,17},{10,2},{18,10},{26,18},{... | collective-permute-start | bytes 196616 | tf_op jit(solution)/shard_map/while/body/eval_jaxpr/ppermute | solution.py:19
  146.4 5.0 %collective-permute-start.1 = (bf16[1,1,128,256]{3,2,1,0:T(8,128)(2,1)S(1)}, bf16[1,1,128,256]{3,2,1,0:T(8,128)(2,1)S(1)}, u32[]{:S(2)}, u32[]{:S(2)}) collective-permute-start(bf16[1,1,128,256]{3,2,1,0:T(8,128)(2,1)S(1)} %get-tuple-element.424), channel_id=1, source_target_pairs={{0,8},{8,16},{16,24},{1,9},{9,17},{17,25},{2,10},{10,18},{18,26},{... | collective-permute-start | bytes 196616 | tf_op jit(solution)/shard_map/while/body/eval_jaxpr/ppermute | solution.py:17
  154.7 15.3 %collective-permute-start.2 = (bf16[1,2,128,1024]{3,2,1,0:T(8,128)(2,1)S(1)}, bf16[1,2,128,1024]{3,2,1,0:T(8,128)(2,1)S(1)}, u32[]{:S(2)}, u32[]{:S(2)}) collective-permute-start(bf16[1,2,128,1024]{3,2,1,0:T(8,128)(2,1)S(1)} %bitcast.157), channel_id=1, source_target_pairs={{0,1},{1,2},{2,3},{3,4},{4,5},{5,6},{6,7},{8,9},{9,10},{10,11},{11... | collective-permute-start | bytes 1572872 | tf_op jit(solution)/shard_map/while/body/eval_jaxpr/ppermute | solution.py:29
  172.5 5.7 %collective-permute-start = (bf16[1,1,128,256]{3,2,1,0:T(8,128)(2,1)S(1)}, bf16[1,1,128,256]{3,2,1,0:T(8,128)(2,1)S(1)}, u32[]{:S(2)}, u32[]{:S(2)}) collective-permute-start(bf16[1,1,128,256]{3,2,1,0:T(8,128)(2,1)S(1)} %get-tuple-element.423), channel_id=1, source_target_pairs={{8,0},{16,8},{24,16},{9,1},{17,9},{25,17},{10,2},{18,10},{26,18},{... | collective-permute-start | bytes 196616 | tf_op jit(solution)/shard_map/while/body/eval_jaxpr/ppermute | solution.py:19
  174.4 5.0 %collective-permute-start.1 = (bf16[1,1,128,256]{3,2,1,0:T(8,128)(2,1)S(1)}, bf16[1,1,128,256]{3,2,1,0:T(8,128)(2,1)S(1)}, u32[]{:S(2)}, u32[]{:S(2)}) collective-permute-start(bf16[1,1,128,256]{3,2,1,0:T(8,128)(2,1)S(1)} %get-tuple-element.424), channel_id=1, source_target_pairs={{0,8},{8,16},{16,24},{1,9},{9,17},{17,25},{2,10},{10,18},{18,26},{... | collective-permute-start | bytes 196616 | tf_op jit(solution)/shard_map/while/body/eval_jaxpr/ppermute | solution.py:17
  182.7 15.2 %collective-permute-start.2 = (bf16[1,2,128,1024]{3,2,1,0:T(8,128)(2,1)S(1)}, bf16[1,2,128,1024]{3,2,1,0:T(8,128)(2,1)S(1)}, u32[]{:S(2)}, u32[]{:S(2)}) collective-permute-start(bf16[1,2,128,1024]{3,2,1,0:T(8,128)(2,1)S(1)} %bitcast.157), channel_id=1, source_target_pairs={{0,1},{1,2},{2,3},{3,4},{4,5},{5,6},{6,7},{8,9},{9,10},{10,11},{11... | collective-permute-start | bytes 1572872 | tf_op jit(solution)/shard_map/while/body/eval_jaxpr/ppermute | solution.py:29
  200.4 5.7 %collective-permute-start = (bf16[1,1,128,256]{3,2,1,0:T(8,128)(2,1)S(1)}, bf16[1,1,128,256]{3,2,1,0:T(8,128)(2,1)S(1)}, u32[]{:S(2)}, u32[]{:S(2)}) collective-permute-start(bf16[1,1,128,256]{3,2,1,0:T(8,128)(2,1)S(1)} %get-tuple-element.423), channel_id=1, source_target_pairs={{8,0},{16,8},{24,16},{9,1},{17,9},{25,17},{10,2},{18,10},{26,18},{... | collective-permute-start | bytes 196616 | tf_op jit(solution)/shard_map/while/body/eval_jaxpr/ppermute | solution.py:19
  202.3 5.1 %collective-permute-start.1 = (bf16[1,1,128,256]{3,2,1,0:T(8,128)(2,1)S(1)}, bf16[1,1,128,256]{3,2,1,0:T(8,128)(2,1)S(1)}, u32[]{:S(2)}, u32[]{:S(2)}) collective-permute-start(bf16[1,1,128,256]{3,2,1,0:T(8,128)(2,1)S(1)} %get-tuple-element.424), channel_id=1, source_target_pairs={{0,8},{8,16},{16,24},{1,9},{9,17},{17,25},{2,10},{10,18},{18,26},{... | collective-permute-start | bytes 196616 | tf_op jit(solution)/shard_map/while/body/eval_jaxpr/ppermute | solution.py:17
  210.7 15.1 %collective-permute-start.2 = (bf16[1,2,128,1024]{3,2,1,0:T(8,128)(2,1)S(1)}, bf16[1,2,128,1024]{3,2,1,0:T(8,128)(2,1)S(1)}, u32[]{:S(2)}, u32[]{:S(2)}) collective-permute-start(bf16[1,2,128,1024]{3,2,1,0:T(8,128)(2,1)S(1)} %bitcast.157), channel_id=1, source_target_pairs={{0,1},{1,2},{2,3},{3,4},{4,5},{5,6},{6,7},{8,9},{9,10},{10,11},{11... | collective-permute-start | bytes 1572872 | tf_op jit(solution)/shard_map/while/body/eval_jaxpr/ppermute | solution.py:29
  228.4 5.8 %collective-permute-start = (bf16[1,1,128,256]{3,2,1,0:T(8,128)(2,1)S(1)}, bf16[1,1,128,256]{3,2,1,0:T(8,128)(2,1)S(1)}, u32[]{:S(2)}, u32[]{:S(2)}) collective-permute-start(bf16[1,1,128,256]{3,2,1,0:T(8,128)(2,1)S(1)} %get-tuple-element.423), channel_id=1, source_target_pairs={{8,0},{16,8},{24,16},{9,1},{17,9},{25,17},{10,2},{18,10},{26,18},{... | collective-permute-start | bytes 196616 | tf_op jit(solution)/shard_map/while/body/eval_jaxpr/ppermute | solution.py:19
  230.3 5.1 %collective-permute-start.1 = (bf16[1,1,128,256]{3,2,1,0:T(8,128)(2,1)S(1)}, bf16[1,1,128,256]{3,2,1,0:T(8,128)(2,1)S(1)}, u32[]{:S(2)}, u32[]{:S(2)}) collective-permute-start(bf16[1,1,128,256]{3,2,1,0:T(8,128)(2,1)S(1)} %get-tuple-element.424), channel_id=1, source_target_pairs={{0,8},{8,16},{16,24},{1,9},{9,17},{17,25},{2,10},{10,18},{18,26},{... | collective-permute-start | bytes 196616 | tf_op jit(solution)/shard_map/while/body/eval_jaxpr/ppermute | solution.py:17
  238.8 15.1 %collective-permute-start.2 = (bf16[1,2,128,1024]{3,2,1,0:T(8,128)(2,1)S(1)}, bf16[1,2,128,1024]{3,2,1,0:T(8,128)(2,1)S(1)}, u32[]{:S(2)}, u32[]{:S(2)}) collective-permute-start(bf16[1,2,128,1024]{3,2,1,0:T(8,128)(2,1)S(1)} %bitcast.157), channel_id=1, source_target_pairs={{0,1},{1,2},{2,3},{3,4},{4,5},{5,6},{6,7},{8,9},{9,10},{10,11},{11... | collective-permute-start | bytes 1572872 | tf_op jit(solution)/shard_map/while/body/eval_jaxpr/ppermute | solution.py:29
  256.3 5.9 %collective-permute-start = (bf16[1,1,128,256]{3,2,1,0:T(8,128)(2,1)S(1)}, bf16[1,1,128,256]{3,2,1,0:T(8,128)(2,1)S(1)}, u32[]{:S(2)}, u32[]{:S(2)}) collective-permute-start(bf16[1,1,128,256]{3,2,1,0:T(8,128)(2,1)S(1)} %get-tuple-element.423), channel_id=1, source_target_pairs={{8,0},{16,8},{24,16},{9,1},{17,9},{25,17},{10,2},{18,10},{26,18},{... | collective-permute-start | bytes 196616 | tf_op jit(solution)/shard_map/while/body/eval_jaxpr/ppermute | solution.py:19
  258.3 5.2 %collective-permute-start.1 = (bf16[1,1,128,256]{3,2,1,0:T(8,128)(2,1)S(1)}, bf16[1,1,128,256]{3,2,1,0:T(8,128)(2,1)S(1)}, u32[]{:S(2)}, u32[]{:S(2)}) collective-permute-start(bf16[1,1,128,256]{3,2,1,0:T(8,128)(2,1)S(1)} %get-tuple-element.424), channel_id=1, source_target_pairs={{0,8},{8,16},{16,24},{1,9},{9,17},{17,25},{2,10},{10,18},{18,26},{... | collective-permute-start | bytes 196616 | tf_op jit(solution)/shard_map/while/body/eval_jaxpr/ppermute | solution.py:17
  266.8 15.0 %collective-permute-start.2 = (bf16[1,2,128,1024]{3,2,1,0:T(8,128)(2,1)S(1)}, bf16[1,2,128,1024]{3,2,1,0:T(8,128)(2,1)S(1)}, u32[]{:S(2)}, u32[]{:S(2)}) collective-permute-start(bf16[1,2,128,1024]{3,2,1,0:T(8,128)(2,1)S(1)} %bitcast.157), channel_id=1, source_target_pairs={{0,1},{1,2},{2,3},{3,4},{4,5},{5,6},{6,7},{8,9},{9,10},{10,11},{11... | collective-permute-start | bytes 1572872 | tf_op jit(solution)/shard_map/while/body/eval_jaxpr/ppermute | solution.py:29
  284.3 5.9 %collective-permute-start = (bf16[1,1,128,256]{3,2,1,0:T(8,128)(2,1)S(1)}, bf16[1,1,128,256]{3,2,1,0:T(8,128)(2,1)S(1)}, u32[]{:S(2)}, u32[]{:S(2)}) collective-permute-start(bf16[1,1,128,256]{3,2,1,0:T(8,128)(2,1)S(1)} %get-tuple-element.423), channel_id=1, source_target_pairs={{8,0},{16,8},{24,16},{9,1},{17,9},{25,17},{10,2},{18,10},{26,18},{... | collective-permute-start | bytes 196616 | tf_op jit(solution)/shard_map/while/body/eval_jaxpr/ppermute | solution.py:19
  286.2 5.3 %collective-permute-start.1 = (bf16[1,1,128,256]{3,2,1,0:T(8,128)(2,1)S(1)}, bf16[1,1,128,256]{3,2,1,0:T(8,128)(2,1)S(1)}, u32[]{:S(2)}, u32[]{:S(2)}) collective-permute-start(bf16[1,1,128,256]{3,2,1,0:T(8,128)(2,1)S(1)} %get-tuple-element.424), channel_id=1, source_target_pairs={{0,8},{8,16},{16,24},{1,9},{9,17},{17,25},{2,10},{10,18},{18,26},{... | collective-permute-start | bytes 196616 | tf_op jit(solution)/shard_map/while/body/eval_jaxpr/ppermute | solution.py:17
  294.8 14.9 %collective-permute-start.2 = (bf16[1,2,128,1024]{3,2,1,0:T(8,128)(2,1)S(1)}, bf16[1,2,128,1024]{3,2,1,0:T(8,128)(2,1)S(1)}, u32[]{:S(2)}, u32[]{:S(2)}) collective-permute-start(bf16[1,2,128,1024]{3,2,1,0:T(8,128)(2,1)S(1)} %bitcast.157), channel_id=1, source_target_pairs={{0,1},{1,2},{2,3},{3,4},{4,5},{5,6},{6,7},{8,9},{9,10},{10,11},{11... | collective-permute-start | bytes 1572872 | tf_op jit(solution)/shard_map/while/body/eval_jaxpr/ppermute | solution.py:29
  312.3 6.0 %collective-permute-start = (bf16[1,1,128,256]{3,2,1,0:T(8,128)(2,1)S(1)}, bf16[1,1,128,256]{3,2,1,0:T(8,128)(2,1)S(1)}, u32[]{:S(2)}, u32[]{:S(2)}) collective-permute-start(bf16[1,1,128,256]{3,2,1,0:T(8,128)(2,1)S(1)} %get-tuple-element.423), channel_id=1, source_target_pairs={{8,0},{16,8},{24,16},{9,1},{17,9},{25,17},{10,2},{18,10},{26,18},{... | collective-permute-start | bytes 196616 | tf_op jit(solution)/shard_map/while/body/eval_jaxpr/ppermute | solution.py:19
  314.2 5.3 %collective-permute-start.1 = (bf16[1,1,128,256]{3,2,1,0:T(8,128)(2,1)S(1)}, bf16[1,1,128,256]{3,2,1,0:T(8,128)(2,1)S(1)}, u32[]{:S(2)}, u32[]{:S(2)}) collective-permute-start(bf16[1,1,128,256]{3,2,1,0:T(8,128)(2,1)S(1)} %get-tuple-element.424), channel_id=1, source_target_pairs={{0,8},{8,16},{16,24},{1,9},{9,17},{17,25},{2,10},{10,18},{18,26},{... | collective-permute-start | bytes 196616 | tf_op jit(solution)/shard_map/while/body/eval_jaxpr/ppermute | solution.py:17
  322.8 14.9 %collective-permute-start.2 = (bf16[1,2,128,1024]{3,2,1,0:T(8,128)(2,1)S(1)}, bf16[1,2,128,1024]{3,2,1,0:T(8,128)(2,1)S(1)}, u32[]{:S(2)}, u32[]{:S(2)}) collective-permute-start(bf16[1,2,128,1024]{3,2,1,0:T(8,128)(2,1)S(1)} %bitcast.157), channel_id=1, source_target_pairs={{0,1},{1,2},{2,3},{3,4},{4,5},{5,6},{6,7},{8,9},{9,10},{10,11},{11... | collective-permute-start | bytes 1572872 | tf_op jit(solution)/shard_map/while/body/eval_jaxpr/ppermute | solution.py:29
  340.2 6.1 %collective-permute-start = (bf16[1,1,128,256]{3,2,1,0:T(8,128)(2,1)S(1)}, bf16[1,1,128,256]{3,2,1,0:T(8,128)(2,1)S(1)}, u32[]{:S(2)}, u32[]{:S(2)}) collective-permute-start(bf16[1,1,128,256]{3,2,1,0:T(8,128)(2,1)S(1)} %get-tuple-element.423), channel_id=1, source_target_pairs={{8,0},{16,8},{24,16},{9,1},{17,9},{25,17},{10,2},{18,10},{26,18},{... | collective-permute-start | bytes 196616 | tf_op jit(solution)/shard_map/while/body/eval_jaxpr/ppermute | solution.py:19
  342.2 5.4 %collective-permute-start.1 = (bf16[1,1,128,256]{3,2,1,0:T(8,128)(2,1)S(1)}, bf16[1,1,128,256]{3,2,1,0:T(8,128)(2,1)S(1)}, u32[]{:S(2)}, u32[]{:S(2)}) collective-permute-start(bf16[1,1,128,256]{3,2,1,0:T(8,128)(2,1)S(1)} %get-tuple-element.424), channel_id=1, source_target_pairs={{0,8},{8,16},{16,24},{1,9},{9,17},{17,25},{2,10},{10,18},{18,26},{... | collective-permute-start | bytes 196616 | tf_op jit(solution)/shard_map/while/body/eval_jaxpr/ppermute | solution.py:17
  350.9 14.8 %collective-permute-start.2 = (bf16[1,2,128,1024]{3,2,1,0:T(8,128)(2,1)S(1)}, bf16[1,2,128,1024]{3,2,1,0:T(8,128)(2,1)S(1)}, u32[]{:S(2)}, u32[]{:S(2)}) collective-permute-start(bf16[1,2,128,1024]{3,2,1,0:T(8,128)(2,1)S(1)} %bitcast.157), channel_id=1, source_target_pairs={{0,1},{1,2},{2,3},{3,4},{4,5},{5,6},{6,7},{8,9},{9,10},{10,11},{11... | collective-permute-start | bytes 1572872 | tf_op jit(solution)/shard_map/while/body/eval_jaxpr/ppermute | solution.py:29
  368.2 6.1 %collective-permute-start = (bf16[1,1,128,256]{3,2,1,0:T(8,128)(2,1)S(1)}, bf16[1,1,128,256]{3,2,1,0:T(8,128)(2,1)S(1)}, u32[]{:S(2)}, u32[]{:S(2)}) collective-permute-start(bf16[1,1,128,256]{3,2,1,0:T(8,128)(2,1)S(1)} %get-tuple-element.423), channel_id=1, source_target_pairs={{8,0},{16,8},{24,16},{9,1},{17,9},{25,17},{10,2},{18,10},{26,18},{... | collective-permute-start | bytes 196616 | tf_op jit(solution)/shard_map/while/body/eval_jaxpr/ppermute | solution.py:19
  370.1 5.5 %collective-permute-start.1 = (bf16[1,1,128,256]{3,2,1,0:T(8,128)(2,1)S(1)}, bf16[1,1,128,256]{3,2,1,0:T(8,128)(2,1)S(1)}, u32[]{:S(2)}, u32[]{:S(2)}) collective-permute-start(bf16[1,1,128,256]{3,2,1,0:T(8,128)(2,1)S(1)} %get-tuple-element.424), channel_id=1, source_target_pairs={{0,8},{8,16},{16,24},{1,9},{9,17},{17,25},{2,10},{10,18},{18,26},{... | collective-permute-start | bytes 196616 | tf_op jit(solution)/shard_map/while/body/eval_jaxpr/ppermute | solution.py:17
  378.9 14.8 %collective-permute-start.2 = (bf16[1,2,128,1024]{3,2,1,0:T(8,128)(2,1)S(1)}, bf16[1,2,128,1024]{3,2,1,0:T(8,128)(2,1)S(1)}, u32[]{:S(2)}, u32[]{:S(2)}) collective-permute-start(bf16[1,2,128,1024]{3,2,1,0:T(8,128)(2,1)S(1)} %bitcast.157), channel_id=1, source_target_pairs={{0,1},{1,2},{2,3},{3,4},{4,5},{5,6},{6,7},{8,9},{9,10},{10,11},{11... | collective-permute-start | bytes 1572872 | tf_op jit(solution)/shard_map/while/body/eval_jaxpr/ppermute | solution.py:29
  396.2 6.2 %collective-permute-start = (bf16[1,1,128,256]{3,2,1,0:T(8,128)(2,1)S(1)}, bf16[1,1,128,256]{3,2,1,0:T(8,128)(2,1)S(1)}, u32[]{:S(2)}, u32[]{:S(2)}) collective-permute-start(bf16[1,1,128,256]{3,2,1,0:T(8,128)(2,1)S(1)} %get-tuple-element.423), channel_id=1, source_target_pairs={{8,0},{16,8},{24,16},{9,1},{17,9},{25,17},{10,2},{18,10},{26,18},{... | collective-permute-start | bytes 196616 | tf_op jit(solution)/shard_map/while/body/eval_jaxpr/ppermute | solution.py:19
  398.1 5.5 %collective-permute-start.1 = (bf16[1,1,128,256]{3,2,1,0:T(8,128)(2,1)S(1)}, bf16[1,1,128,256]{3,2,1,0:T(8,128)(2,1)S(1)}, u32[]{:S(2)}, u32[]{:S(2)}) collective-permute-start(bf16[1,1,128,256]{3,2,1,0:T(8,128)(2,1)S(1)} %get-tuple-element.424), channel_id=1, source_target_pairs={{0,8},{8,16},{16,24},{1,9},{9,17},{17,25},{2,10},{10,18},{18,26},{... | collective-permute-start | bytes 196616 | tf_op jit(solution)/shard_map/while/body/eval_jaxpr/ppermute | solution.py:17
  406.9 14.7 %collective-permute-start.2 = (bf16[1,2,128,1024]{3,2,1,0:T(8,128)(2,1)S(1)}, bf16[1,2,128,1024]{3,2,1,0:T(8,128)(2,1)S(1)}, u32[]{:S(2)}, u32[]{:S(2)}) collective-permute-start(bf16[1,2,128,1024]{3,2,1,0:T(8,128)(2,1)S(1)} %bitcast.157), channel_id=1, source_target_pairs={{0,1},{1,2},{2,3},{3,4},{4,5},{5,6},{6,7},{8,9},{9,10},{10,11},{11... | collective-permute-start | bytes 1572872 | tf_op jit(solution)/shard_map/while/body/eval_jaxpr/ppermute | solution.py:29
where the time goes:
time: 429 us; the launch traced here: 422 us
  waiting for transfers between devices  193 us (45%)
  starting transfers between devices  106 us (25%)
  matrix products  65.7 us (15%)
  other arithmetic  50.3 us (12%)
  local copies, waits for them, and re-layouts  4.41 us (1%)
    ppermute x15, waiting for transfers between devices, passed_along(): lax.ppermute(value, axis, [(source, source + steps) for source in range(l...  174 us
    ppermute x15, starting transfers between devices, extended(): lax.ppermute(tail, axis, [(i, (i + 1) % count) for i in range(ends)])  56.5 us
    dynamic_update_slice x15, other arithmetic, one_step(): lax.dynamic_update_slice_in_dim(result, jnp.where(active, produced, curre...  30.5 us
    ppermute x15, starting transfers between devices, extended(): lax.ppermute(head, axis, [((i + 1) % count, i) for i in range(ends)])  29.6 us
    dot_general x15, matrix products, finish_block(): jnp.dot(spatial, w_three, preferred_element_type=jnp.float32)  23.1 us
    dot_general x120, matrix products, finish_block(): jnp.dot(window, w_two[row_off, col_off], preferred_element_type=jnp.float32)  22.4 us
    dot_general x15, matrix products, reduce_part(): jnp.dot(maps.reshape(-1, chans), w_one, preferred_element_type=jnp.float32)  20.2 us
    ppermute x15, starting transfers between devices, passed_along(): lax.ppermute(value, axis, [(source, source + steps) for source in range(l...  19.4 us
  transfers between devices with their start and end apart: 45, of which 30 were waited for; matrix products, arithmetic and copies ran while one was open for 7% of the time, Pallas kernels for 0%

commit v1 on v0

v1 whole, which is shorter than its diff:
```python
import functools

import jax
import jax.numpy as jnp
from jax import lax
from jax.experimental import pallas as pl
from jax.experimental.pallas import tpu as pltpu
from jax.sharding import PartitionSpec as P

TILE_W = 8
F32 = jnp.float32
BF16 = jnp.bfloat16


def tissue_mask(tile_list, rows):
    tiles_count = tile_list.shape[-1]
    columns = jnp.arange(tiles_count, dtype=jnp.int32)
    hits = jnp.any(tile_list[..., :, None] == columns[None, None, None, :], axis=-2)
    tissue = hits.astype(jnp.float32)
    tissue = jnp.repeat(tissue, rows, axis=1)
    return jnp.repeat(tissue, TILE_W, axis=2)


def kernel(
    strips, sections, half, cols, chans, inner,
    feat, mask, w1, w2, w3, bias, out,
    inbuf, mid, fin, stage, halo, v1, v2, v3, vb,
    feat_sem, own_sem, in_sem, fwd_sem, loc_sem, out_send, out_recv,
    halo_send, halo_recv, w_send, w_recv, m_send, m_recv,
):
    p = lax.axis_index("strip")
    s = lax.axis_index("section")
    pair = s // 2
    b = s % 2
    c = p % 2
    pairs = sections // 2
    partner = {"section": s + 1 - 2 * b}
    mate = {"strip": p + 1 - 2 * c}
    up, down = {"strip": p - 1}, {"strip": p + 1}
    ahead, behind = {"section": s + 2}, {"section": s - 2}
    has_up, has_down = p > 0, p < strips - 1
    first, last = pair == 0, pair == pairs - 1
    MESH = pl.DeviceIdType.MESH

    def remote(src, dst, send, recv, to):
        return pltpu.make_async_remote_copy(
            src_ref=src, dst_ref=dst, send_sem=send, recv_sem=recv, device_id=to, device_id_type=MESH
        )

    barrier = pltpu.get_barrier_semaphore()

    def greet(to):
        pl.semaphore_signal(barrier, inc=1, device_id=to, device_id_type=MESH)

    greet(partner)
    pl.when(has_up)(lambda: greet(up))
    pl.when(has_down)(lambda: greet(down))
    pl.when(jnp.logical_not(last))(lambda: greet(ahead))
    pl.when(jnp.logical_not(first))(lambda: greet(behind))

    weights = ((w1, v1), (w2, v2), (w3, v3))

    def own_copies():
        made = [pltpu.make_async_copy(w, v.at[b], own_sem.at[i]) for i, (w, v) in enumerate(weights)]
        return made + [pltpu.make_async_copy(bias, vb.at[b], own_sem.at[3])]

    def feat_copy(j):
        return pltpu.make_async_copy(feat.at[b * half + j], inbuf.at[j], feat_sem.at[j])

    for one in own_copies():
        one.start()

    @pl.when(first)
    def _():
        for j in range(half):
            feat_copy(j).start()

    def zero_edge(side):
        def body(t, carry):
            halo[t, side] = jnp.zeros((cols, inner), BF16)
            return carry

        lax.fori_loop(0, 2 * half, body, 0)

    pl.when(jnp.logical_not(has_up))(lambda: zero_edge(0))
    pl.when(jnp.logical_not(has_down))(lambda: zero_edge(1))

    peers = 1 + sum(jnp.where(met, 1, 0) for met in (has_up, has_down, pair < pairs - 1, pair > 0))
    pl.semaphore_wait(barrier, peers)

    def part_copies():
        made = []
        for i, (w, v) in enumerate(weights):
            depth = w.shape[0] // 2
            rows = pl.ds(pl.multiple_of(c * depth, depth), depth)
            made.append(remote(w.at[rows], v.at[b, rows], w_send.at[i], w_recv.at[i], partner))
        made.append(remote(bias, vb.at[b], w_send.at[3], w_recv.at[3], partner))
        return made

    def mate_copies():
        made = []
        for i, (w, v) in enumerate(weights):
            depth = w.shape[0] // 2
            rows = pl.ds(pl.multiple_of(c * depth, depth), depth)
            where = v.at[1 - b, rows]
            made.append(remote(where, where, m_send.at[i], m_recv.at[i], mate))
        return made

    for i in (3, 0, 1, 2):
        part_copies()[i].start()

    def wait_own():
        for one in own_copies():
            one.wait()

    def wait_other():
        part_copies()[3].wait_recv()
        for i in range(3):
            part_copies()[i].wait_recv()
            mate_copies()[i].start()
        for i in range(3):
            mate_copies()[i].wait_recv()

    def halo_up(t):
        return remote(
            stage.at[t, pl.ds(0, cols)], halo.at[t, 1], halo_send.at[t, 0], halo_recv.at[t, 1], up
        )

    def halo_down(t):
        return remote(
            stage.at[t, pl.ds(cols, cols)], halo.at[t, 0], halo_send.at[t, 1], halo_recv.at[t, 0], down
        )

    column = lax.broadcasted_iota(jnp.int32, (2 * cols, inner), 0) % cols

    def dot(lhs, rhs):
        return jnp.dot(lhs, rhs, preferred_element_type=F32)

    def block(which, j, src, dst):
        t = which * half + j
        reduced = dot(src[j], v1[which]) + vb[which, 0:1, 0:inner]
        stage[t] = jnp.maximum(reduced, 0.0).astype(BF16)
        pl.when(has_up)(lambda: halo_up(t).start())
        pl.when(has_down)(lambda: halo_down(t).start())

        def tap(dy, dx):
            return v2[which, pl.ds((dy * 3 + dx) * inner, inner), :]

        both = stage[t]
        upper, lower = both[:cols], both[cols:]
        sums = []
        for dx in range(3):
            centre = dot(both, tap(1, dx))
            cross = jnp.concatenate([dot(lower, tap(2, dx)), dot(upper, tap(0, dx))], axis=0)
            sums.append(centre + cross)
        pl.when(has_up)(lambda: halo_down(t).wait_recv())
        pl.when(has_down)(lambda: halo_up(t).wait_recv())
        above, below = halo[t, 0], halo[t, 1]
        for dx in range(3):
            sums[dx] += jnp.concatenate([dot(above, tap(0, dx)), dot(below, tap(2, dx))], axis=0)
        left = jnp.where(column == 0, 0.0, pltpu.roll(sums[0], 1, 0))
        right = jnp.where(column == cols - 1, 0.0, pltpu.roll(sums[2], 2 * cols - 1, 0))
        total = sums[1] + left + right + vb[which, 1:2, 0:inner]
        spatial = jnp.maximum(total, 0.0).astype(BF16)
        kept = mask[b * half + j][:, 0:1]
        for low in range(0, chans, inner):
            span = pl.ds(low, inner)
            value = src[j, :, span].astype(F32) + dot(spatial, v3[which, :, span]) + vb[which, 2:3, span]
            dst[j, :, span] = (jnp.maximum(value, 0.0) * kept).astype(BF16)

    def in_copy(j):
        return remote(fin.at[j], inbuf.at[j], fwd_sem.at[j], in_sem.at[j], ahead)

    def out_local(buffer, j):
        return pltpu.make_async_copy(buffer.at[j], out.at[b * half + j], loc_sem.at[j])

    def out_remote(buffer, j):
        return remote(buffer.at[j], out.at[b * half + j], out_send.at[j], out_recv.at[j], partner)

    pl.when(b == 0)(wait_own)
    pl.when(b == 1)(wait_other)

    def one_slide(j, carry):
        pl.when(first)(lambda: feat_copy(j).wait())
        pl.when(jnp.logical_not(first))(lambda: in_copy(j).wait_recv())
        block(0, j, inbuf, mid)
        pl.when(b == 0)(lambda: out_local(mid, j).start())
        pl.when(b == 1)(lambda: out_remote(mid, j).start())

        @pl.when(j == 0)
        def _():
            pl.when(b == 0)(wait_other)
            pl.when(b == 1)(wait_own)

        block(1, j, mid, fin)
        pl.when(jnp.logical_not(last))(lambda: in_copy(j).start())
        pl.when(b == 1)(lambda: out_local(fin, j).start())
        pl.when(b == 0)(lambda: out_remote(fin, j).start())
        return carry

    lax.fori_loop(0, half, one_slide, 0)

    for one in part_copies() + mate_copies():
        one.wait_send()

    def drain(j, carry):
        for t in (j, half + j):
            pl.when(has_up)(lambda t=t: halo_up(t).wait_send())
            pl.when(has_down)(lambda t=t: halo_down(t).wait_send())
        pl.when(jnp.logical_not(last))(lambda: in_copy(j).wait_send())
        out_local(mid, j).wait()
        out_remote(mid, j).wait()
        return carry

    lax.fori_loop(0, half, drain, 0)


def shards(
    strips, sections,
    features, tile_list, w_reduce, bias_reduce, w_spatial, bias_spatial, w_expand, bias_expand,
):
    slides, rows, cols, chans = features.shape
    inner = w_reduce.shape[-1]
    half = slides // 2
    cells = rows * cols
    tissue = tissue_mask(tile_list, rows).reshape(slides, cells, 1)
    mask = jnp.broadcast_to(tissue, (slides, cells, 128))
    bias = jnp.zeros((8, chans), F32)
    bias = bias.at[0, :inner].set(bias_reduce[0].astype(F32))
    bias = bias.at[1, :inner].set(bias_spatial[0].astype(F32))
    bias = bias.at[2].set(bias_expand[0].astype(F32))
    dma = pltpu.SemaphoreType.DMA
    anywhere = pl.BlockSpec(memory_space=pl.ANY)
    result = pl.pallas_call(
        functools.partial(kernel, strips, sections, half, cols, chans, inner),
        out_shape=jax.ShapeDtypeStruct((slides, cells, chans), BF16),
        in_specs=[anywhere, pl.BlockSpec(memory_space=pltpu.VMEM)] + [anywhere] * 4,
        out_specs=anywhere,
        scratch_shapes=[
            pltpu.VMEM((half, cells, chans), BF16),
            pltpu.VMEM((half, cells, chans), BF16),
            pltpu.VMEM((half, cells, chans), BF16),
            pltpu.VMEM((2 * half, cells, inner), BF16),
            pltpu.VMEM((2 * half, 2, cols, inner), BF16),
            pltpu.VMEM((2, chans, inner), BF16),
            pltpu.VMEM((2, 9 * inner, inner), BF16),
            pltpu.VMEM((2, inner, chans), BF16),
            pltpu.VMEM((2, 8, chans), F32),
            dma((half,)), dma((4,)), dma((half,)), dma((half,)), dma((half,)), dma((half,)), dma((half,)),
            dma((2 * half, 2)), dma((2 * half, 2)), dma((4,)), dma((4,)), dma((3,)), dma((3,)),
        ],
        compiler_params=pltpu.CompilerParams(
            collective_id=0, has_side_effects=True, vmem_limit_bytes=40 * 1024 * 1024
        ),
    )(
        features.reshape(slides, cells, chans),
        mask,
        w_reduce[0],
        w_spatial.reshape(9 * inner, inner),
        w_expand[0],
        bias,
    )
    return result.reshape(1, slides, rows, cols, chans)


def solution(mesh):
    in_specs = (
        P(None, "strip", None, None),
        P(None, "strip", None),
        P("section", None, None),
        P("section", None),
        P("section", None, None, None, None),
        P("section", None),
        P("section", None, None),
        P("section", None),
    )
    out_specs = P("section", None, "strip", None, None)
    body = functools.partial(shards, mesh.shape["strip"], mesh.shape["section"])
    return jax.shard_map(body, mesh=mesh, in_specs=in_specs, out_specs=out_specs, check_vma=False)
```

time: 429 us -> 158 us (0.37); the launches traced: 422 us -> 158 us
  waiting for transfers between devices: 193 us -> 0 us
  Pallas kernels: 0 us -> 146 us
  starting transfers between devices: 106 us -> 0 us
  matrix products: 65.7 us -> 0 us
  other arithmetic: 50.3 us -> 2.85 us
    ppermute x45 -> x0, waiting for transfers between devices: 193 us -> none  [the longest x15 174 us: passed_along(): lax.ppermute(value, axis, [(source, source + steps) for source in range(l...]
    pallas_call x0 -> x1, Pallas kernels: none -> 146 us  [shards(): pl.pallas_call(functools.partial(kernel, strips, sections, half, cols, ch...]
    ppermute x45 -> x0, starting transfers between devices: 106 us -> none  [the longest x15 56.5 us: extended(): lax.ppermute(tail, axis, [(i, (i + 1) % count) for i in range(ends)])]
    dot_general x150 -> x0, matrix products: 65.7 us -> none  [the longest x15 23.1 us: finish_block(): jnp.dot(spatial, w_three, preferred_element_type=jnp.float32)]
    dynamic_update_slice x15 -> x0, other arithmetic: 30.5 us -> none  [one_step(): lax.dynamic_update_slice_in_dim(result, jnp.where(active, produced, curre...]
    select_n x15 -> x0, other arithmetic: 17.2 us -> none  [one_step(): inputs_now = jnp.where(section_index == 0, first, carried)]
    unnamed x8 -> x9, local copies, waits for them, and re-layouts: 0.03 us -> 7.55 us
  transfers between devices with their start and end apart: 45 -> 0, of which waited for: 30 -> 0; matrix products, arithmetic and copies ran while one was open for 7% -> 0% of each run, Pallas kernels for 0% -> 0%
where the time goes in v1:
time: 158 us
  Pallas kernels  146 us (92%)
  local copies, waits for them, and re-layouts  8.34 us (5%)
  other arithmetic  2.85 us (2%)
    pallas_call x1, Pallas kernels, shards(): pl.pallas_call(functools.partial(kernel, strips, sections, half, cols, ch...  146 us
    unnamed x9, local copies, waits for them, and re-layouts  7.55 us

profile of v1, /device:TPU:29, one launch (start us, length us, event | category | flops | bytes accessed | tf_op | source)
XLA Modules:
  0.0 157.7 jit_solution(8794584986128447090)
XLA Ops:
  0.0 0.8 fusion
  0.8 0.7 convert_element_type.17
  1.5 0.7 convert_element_type.18
  2.2 0.7 pad_convert_fusion
  2.9 0.2 scatter.19
  3.0 0.1 scatter.20.bias
  3.1 0.1 broadcast_in_dim.6
  3.2 0.1 broadcast_in_dim.7
  3.3 0.3 broadcast_in_dim.16.mask
  3.7 0.0 copy-start
  3.7 2.2 %copy-done = bf16[8,2,128,1024]{3,2,1,0:T(8,128)(2,1)S(1)} copy-done((bf16[8,2,128,1024]{3,2,1,0:T(8,128)(2,1)S(1)}, bf16[8,2,128,1024]{3,2,1,0:T(8,128)(2,1)}, u32[]{:S(2)}) %copy-start) | copy-done | bytes 4194328
  5.9 0.0 copy-start.1
  5.9 1.3 copy-done.1
  7.1 0.0 copy-start.2
  7.1 1.0 copy-done.2
  8.2 0.0 copy-start.3
  8.2 1.0 copy-done.3
  9.2 146.5 %shard_map.82 = bf16[8,256,1024]{2,1,0:T(8,128)(2,1)S(1)} custom-call(bf16[8,256,1024]{2,1,0:T(8,128)(2,1)S(1)} %bitcast.9, f32[8,256,128]{2,1,0:T(8,128)S(1)} %broadcast_in_dim.16.mask, bf16[1024,256]{1,0:T(8,128)(2,1)S(1)} %bitcast.11, bf16[2304,256]{1,0:T(8,128)(2,1)S(1)} %bitcast.10, bf16[256,1024]{1,0:T(8,128)(2,1)S(1)} %bitcast.12, ...), custom_call_target="tpu_custom_call" | custom-call | tf_op jit(solution)/shard_map/pallas_call | solution.py:234
  155.7 2.0 %copy.12 = bf16[1,8,2,128,1024]{4,3,2,1,0:T(8,128)(2,1)} copy(bf16[1,8,2,128,1024]{4,3,2,1,0:T(8,128)(2,1)S(1)} %bitcast.8) | data formatting | bytes 8388608
  (1 shorter events, 0.0 us)
Async XLA Ops:
  3.7 2.2 %copy-start = (bf16[8,2,128,1024]{3,2,1,0:T(8,128)(2,1)S(1)}, bf16[8,2,128,1024]{3,2,1,0:T(8,128)(2,1)}, u32[]{:S(2)}) copy-start(bf16[8,2,128,1024]{3,2,1,0:T(8,128)(2,1)} %param.14) | copy-start | bytes 12582916
  5.9 1.3 copy-start.1
  7.1 1.0 copy-start.2
  8.2 1.0 copy-start.3

commit v2 on v1

--- a/solution.py
+++ b/solution.py
@@ -33,9 +33,12 @@
     pair = s // 2
     b = s % 2
     c = p % 2
+    q = p % 4
+    side = q // 2
     pairs = sections // 2
     partner = {"section": s + 1 - 2 * b}
     mate = {"strip": p + 1 - 2 * c}
+    across = {"strip": p + 2 - 4 * side}
     up, down = {"strip": p - 1}, {"strip": p + 1}
     ahead, behind = {"section": s + 2}, {"section": s - 2}
     has_up, has_down = p > 0, p < strips - 1
@@ -53,6 +56,7 @@
         pl.semaphore_signal(barrier, inc=1, device_id=to, device_id_type=MESH)
 
     greet(partner)
+    greet(across)
     pl.when(has_up)(lambda: greet(up))
     pl.when(has_down)(lambda: greet(down))
     pl.when(jnp.logical_not(last))(lambda: greet(ahead))
@@ -75,9 +79,9 @@
         for j in range(half):
             feat_copy(j).start()
 
-    def zero_edge(side):
+    def zero_edge(edge):
         def body(t, carry):
-            halo[t, side] = jnp.zeros((cols, inner), BF16)
+            halo[t, edge] = jnp.zeros((cols, inner), BF16)
             return carry
 
         lax.fori_loop(0, 2 * half, body, 0)
@@ -85,41 +89,55 @@
     pl.when(jnp.logical_not(has_up))(lambda: zero_edge(0))
     pl.when(jnp.logical_not(has_down))(lambda: zero_edge(1))
 
-    peers = 1 + sum(jnp.where(met, 1, 0) for met in (has_up, has_down, pair < pairs - 1, pair > 0))
+    peers = 2 + sum(jnp.where(met, 1, 0) for met in (has_up, has_down, pair < pairs - 1, pair > 0))
     pl.semaphore_wait(barrier, peers)
 
-    def part_copies():
-        made = []
-        for i, (w, v) in enumerate(weights):
-            depth = w.shape[0] // 2
-            rows = pl.ds(pl.multiple_of(c * depth, depth), depth)
-            made.append(remote(w.at[rows], v.at[b, rows], w_send.at[i], w_recv.at[i], partner))
-        made.append(remote(bias, vb.at[b], w_send.at[3], w_recv.at[3], partner))
-        return made
-
-    def mate_copies():
-        made = []
-        for i, (w, v) in enumerate(weights):
-            depth = w.shape[0] // 2
-            rows = pl.ds(pl.multiple_of(c * depth, depth), depth)
-            where = v.at[1 - b, rows]
-            made.append(remote(where, where, m_send.at[i], m_recv.at[i], mate))
-        return made
+    def quarter(i, which):
+        depth = weights[i][0].shape[0] // 4
+        return pl.ds(pl.multiple_of(which * depth, depth), depth)
+
+    def part_copy(i):
+        if i == 3:
+            return remote(bias, vb.at[b], w_send.at[3], w_recv.at[3], partner)
+        w, v = weights[i]
+        rows = quarter(i, q)
+        return remote(w.at[rows], v.at[b, rows], w_send.at[i], w_recv.at[i], partner)
+
+    def spread(i, which, slot, to):
+        where = weights[i][1].at[1 - b, quarter(i, which)]
+        return remote(where, where, m_send.at[slot, i], m_recv.at[slot, i], to)
+
+    def mate_copy(i):
+        return spread(i, q, 0, mate)
+
+    def across_copy(i):
+        return spread(i, q, 1, across)
+
+    def onward_copy(i):
+        return spread(i, (q + 2) % 4, 2, mate)
 
     for i in (3, 0, 1, 2):
-        part_copies()[i].start()
+        part_copy(i).start()
 
     def wait_own():
         for one in own_copies():
             one.wait()
 
     def wait_other():
-        part_copies()[3].wait_recv()
+        part_copy(3).wait_recv()
+        part_copy(0).wait_recv()
+        across_copy(0).start()
+        mate_copy(0).start()
         for i in range(3):
-            part_copies()[i].wait_recv()
-            mate_copies()[i].start()
+            if i < 2:
+                part_copy(i + 1).wait_recv()
+                across_copy(i + 1).start()
+                mate_copy(i + 1).start()
+            across_copy(i).wait_recv()
+            onward_copy(i).start()
         for i in range(3):
-            mate_copies()[i].wait_recv()
+            mate_copy(i).wait_recv()
+            onward_copy(i).wait_recv()
 
     def halo_up(t):
         return remote(
@@ -136,12 +154,16 @@
     def dot(lhs, rhs):
         return jnp.dot(lhs, rhs, preferred_element_type=F32)
 
-    def block(which, j, src, dst):
+    def block(which, j, src, dst, arrived, finished):
         t = which * half + j
-        reduced = dot(src[j], v1[which]) + vb[which, 0:1, 0:inner]
-        stage[t] = jnp.maximum(reduced, 0.0).astype(BF16)
-        pl.when(has_up)(lambda: halo_up(t).start())
-        pl.when(has_down)(lambda: halo_down(t).start())
+        for r in range(2):
+            arrived(r)
+            reduced = dot(src[j, pl.ds(r * cols, cols)], v1[which]) + vb[which, 0:1, 0:inner]
+            stage[t, pl.ds(r * cols, cols)] = jnp.maximum(reduced, 0.0).astype(BF16)
+            if r == 0:
+                pl.when(has_up)(lambda: halo_up(t).start())
+            else:
+                pl.when(has_down)(lambda: halo_down(t).start())
 
         def tap(dy, dx):
             return v2[which, pl.ds((dy * 3 + dx) * inner, inner), :]
@@ -162,14 +184,21 @@
         right = jnp.where(column == cols - 1, 0.0, pltpu.roll(sums[2], 2 * cols - 1, 0))
         total = sums[1] + left + right + vb[which, 1:2, 0:inner]
         spatial = jnp.maximum(total, 0.0).astype(BF16)
-        kept = mask[b * half + j][:, 0:1]
-        for low in range(0, chans, inner):
-            span = pl.ds(low, inner)
-            value = src[j, :, span].astype(F32) + dot(spatial, v3[which, :, span]) + vb[which, 2:3, span]
-            dst[j, :, span] = (jnp.maximum(value, 0.0) * kept).astype(BF16)
-
-    def in_copy(j):
-        return remote(fin.at[j], inbuf.at[j], fwd_sem.at[j], in_sem.at[j], ahead)
+        for r in range(2):
+            part = pl.ds(r * cols, cols)
+            kept = mask[b * half + j, part, 0:1]
+            for low in range(0, chans, inner):
+                span = pl.ds(low, inner)
+                value = dot(spatial[r * cols : (r + 1) * cols], v3[which, :, span])
+                value += src[j, part, span].astype(F32) + vb[which, 2:3, span]
+                dst[j, part, span] = (jnp.maximum(value, 0.0) * kept).astype(BF16)
+            finished(r)
+
+    def in_copy(j, r):
+        part = pl.ds(r * cols, cols)
+        return remote(
+            fin.at[j, part], inbuf.at[j, part], fwd_sem.at[j, r], in_sem.at[j, r], ahead
+        )
 
     def out_local(buffer, j):
         return pltpu.make_async_copy(buffer.at[j], out.at[b * half + j], loc_sem.at[j])
@@ -182,8 +211,17 @@
 
     def one_slide(j, carry):
         pl.when(first)(lambda: feat_copy(j).wait())
-        pl.when(jnp.logical_not(first))(lambda: in_copy(j).wait_recv())
-        block(0, j, inbuf, mid)
+
+        def arrived(r):
+            pl.when(jnp.logical_not(first))(lambda: in_copy(j, r).wait_recv())
+
+        def finished(r):
+            pl.when(jnp.logical_not(last))(lambda: in_copy(j, r).start())
+
+        def nothing(r):
+            pass
+
+        block(0, j, inbuf, mid, arrived, nothing)
         pl.when(b == 0)(lambda: out_local(mid, j).start())
         pl.when(b == 1)(lambda: out_remote(mid, j).start())
 
@@ -192,22 +230,26 @@
             pl.when(b == 0)(wait_other)
             pl.when(b == 1)(wait_own)
 
-        block(1, j, mid, fin)
-        pl.when(jnp.logical_not(last))(lambda: in_copy(j).start())
+        block(1, j, mid, fin, nothing, finished)
         pl.when(b == 1)(lambda: out_local(fin, j).start())
         pl.when(b == 0)(lambda: out_remote(fin, j).start())
         return carry
 
     lax.fori_loop(0, half, one_slide, 0)
 
-    for one in part_copies() + mate_copies():
-        one.wait_send()
+    part_copy(3).wait_send()
+    for i in range(3):
+        part_copy(i).wait_send()
+        mate_copy(i).wait_send()
+        across_copy(i).wait_send()
+        onward_copy(i).wait_send()
 
     def drain(j, carry):
         for t in (j, half + j):
             pl.when(has_up)(lambda t=t: halo_up(t).wait_send())
             pl.when(has_down)(lambda t=t: halo_down(t).wait_send())
-        pl.when(jnp.logical_not(last))(lambda: in_copy(j).wait_send())
+        for r in range(2):
+            pl.when(jnp.logical_not(last))(lambda r=r: in_copy(j, r).wait_send())
         out_local(mid, j).wait()
         out_remote(mid, j).wait()
         return carry
@@ -246,11 +288,11 @@
             pltpu.VMEM((2, 9 * inner, inner), BF16),
             pltpu.VMEM((2, inner, chans), BF16),
             pltpu.VMEM((2, 8, chans), F32),
-            dma((half,)), dma((4,)), dma((half,)), dma((half,)), dma((half,)), dma((half,)), dma((half,)),
-            dma((2 * half, 2)), dma((2 * half, 2)), dma((4,)), dma((4,)), dma((3,)), dma((3,)),
+            dma((half,)), dma((4,)), dma((half, 2)), dma((half, 2)), dma((half,)), dma((half,)), dma((half,)),
+            dma((2 * half, 2)), dma((2 * half, 2)), dma((4,)), dma((4,)), dma((3, 3)), dma((3, 3)),
         ],
         compiler_params=pltpu.CompilerParams(
-            collective_id=0, has_side_effects=True, vmem_limit_bytes=40 * 1024 * 1024
+            collective_id=0, has_side_effects=True, vmem_limit_bytes=56 * 1024 * 1024
         ),
     )(
         features.reshape(slides, cells, chans),

time: 158 us -> 185 us (1.17)
  Pallas kernels: 146 us -> 174 us
    pallas_call x1, Pallas kernels: 146 us -> 174 us  [shards(): pl.pallas_call(functools.partial(kernel, strips, sections, half, cols, ch...]
    unnamed x9 -> x3, local copies, waits for them, and re-layouts: 7.55 us -> 4.81 us
where the time goes in v2:
time: 185 us; the launch traced here: 184 us
  Pallas kernels  174 us (94%)
  local copies, waits for them, and re-layouts  6.58 us (4%)
  other arithmetic  2.85 us (2%)
    pallas_call x1, Pallas kernels, shards(): pl.pallas_call(functools.partial(kernel, strips, sections, half, cols, ch...  174 us
    unnamed x3, local copies, waits for them, and re-layouts  4.81 us

profile of v2, /device:TPU:29, one launch (start us, length us, event | category | flops | bytes accessed | tf_op | source)
XLA Modules:
  0.0 183.8 jit_solution(16943746822386660126)
XLA Ops:
  0.0 0.8 fusion
  0.8 0.7 convert_element_type.17
  1.5 0.7 convert_element_type.18
  2.2 0.7 pad_convert_fusion
  2.9 0.2 scatter.19
  3.0 0.1 scatter.20.bias
  3.1 0.0 copy-start
  3.1 0.1 broadcast_in_dim.6
  3.2 0.1 broadcast_in_dim.7
  3.3 1.3 broadcast_in_dim.16.mask
  4.7 0.0 copy-done
  4.7 174.3 %shard_map.82 = bf16[8,256,1024]{2,1,0:T(8,128)(2,1)} custom-call(bf16[8,256,1024]{2,1,0:T(8,128)(2,1)} %bitcast.9, f32[8,256,128]{2,1,0:T(8,128)} %broadcast_in_dim.16.mask, bf16[1024,256]{1,0:T(8,128)(2,1)} %bitcast.11, bf16[2304,256]{1,0:T(8,128)(2,1)} %bitcast.10, bf16[256,1024]{1,0:T(8,128)(2,1)} %bitcast.12, f32[8,1024]{1,0:T(8,128)} %copy-done), custom_call_target="tpu_custom_call" | custom-call | tf_op jit(solution)/shard_map/pallas_call | solution.py:276
  179.0 4.8 %copy.12 = bf16[1,8,2,128,1024]{4,3,2,1,0:T(8,128)(2,1)} copy(bf16[1,8,2,128,1024]{4,3,2,1,0:T(8,128)(2,1)} %bitcast.8) | data formatting | bytes 8388608
  (1 shorter events, 0.0 us)
Async XLA Ops:
  3.1 1.5 copy-start

commit v3 on v2

--- a/solution.py
+++ b/solution.py
@@ -154,16 +154,12 @@
     def dot(lhs, rhs):
         return jnp.dot(lhs, rhs, preferred_element_type=F32)
 
-    def block(which, j, src, dst, arrived, finished):
+    def block(which, j, src, dst):
         t = which * half + j
-        for r in range(2):
-            arrived(r)
-            reduced = dot(src[j, pl.ds(r * cols, cols)], v1[which]) + vb[which, 0:1, 0:inner]
-            stage[t, pl.ds(r * cols, cols)] = jnp.maximum(reduced, 0.0).astype(BF16)
-            if r == 0:
-                pl.when(has_up)(lambda: halo_up(t).start())
-            else:
-                pl.when(has_down)(lambda: halo_down(t).start())
+        reduced = dot(src[j], v1[which]) + vb[which, 0:1, 0:inner]
+        stage[t] = jnp.maximum(reduced, 0.0).astype(BF16)
+        pl.when(has_up)(lambda: halo_up(t).start())
+        pl.when(has_down)(lambda: halo_down(t).start())
 
         def tap(dy, dx):
             return v2[which, pl.ds((dy * 3 + dx) * inner, inner), :]
@@ -184,21 +180,14 @@
         right = jnp.where(column == cols - 1, 0.0, pltpu.roll(sums[2], 2 * cols - 1, 0))
         total = sums[1] + left + right + vb[which, 1:2, 0:inner]
         spatial = jnp.maximum(total, 0.0).astype(BF16)
-        for r in range(2):
-            part = pl.ds(r * cols, cols)
-            kept = mask[b * half + j, part, 0:1]
-            for low in range(0, chans, inner):
-                span = pl.ds(low, inner)
-                value = dot(spatial[r * cols : (r + 1) * cols], v3[which, :, span])
-                value += src[j, part, span].astype(F32) + vb[which, 2:3, span]
-                dst[j, part, span] = (jnp.maximum(value, 0.0) * kept).astype(BF16)
-            finished(r)
-
-    def in_copy(j, r):
-        part = pl.ds(r * cols, cols)
-        return remote(
-            fin.at[j, part], inbuf.at[j, part], fwd_sem.at[j, r], in_sem.at[j, r], ahead
-        )
+        kept = mask[b * half + j][:, 0:1]
+        for low in range(0, chans, inner):
+            span = pl.ds(low, inner)
+            value = src[j, :, span].astype(F32) + dot(spatial, v3[which, :, span]) + vb[which, 2:3, span]
+            dst[j, :, span] = (jnp.maximum(value, 0.0) * kept).astype(BF16)
+
+    def in_copy(j):
+        return remote(fin.at[j], inbuf.at[j], fwd_sem.at[j], in_sem.at[j], ahead)
 
     def out_local(buffer, j):
         return pltpu.make_async_copy(buffer.at[j], out.at[b * half + j], loc_sem.at[j])
@@ -211,17 +200,8 @@
 
     def one_slide(j, carry):
         pl.when(first)(lambda: feat_copy(j).wait())
-
-        def arrived(r):
-            pl.when(jnp.logical_not(first))(lambda: in_copy(j, r).wait_recv())
-
-        def finished(r):
-            pl.when(jnp.logical_not(last))(lambda: in_copy(j, r).start())
-
-        def nothing(r):
-            pass
-
-        block(0, j, inbuf, mid, arrived, nothing)
+        pl.when(jnp.logical_not(first))(lambda: in_copy(j).wait_recv())
+        block(0, j, inbuf, mid)
         pl.when(b == 0)(lambda: out_local(mid, j).start())
         pl.when(b == 1)(lambda: out_remote(mid, j).start())
 
@@ -230,7 +210,13 @@
             pl.when(b == 0)(wait_other)
             pl.when(b == 1)(wait_own)
 
-        block(1, j, mid, fin, nothing, finished)
+        block(1, j, mid, fin)
+
+        @pl.when(jnp.logical_not(last))
+        def _():
+            pl.when(j > 0)(lambda: in_copy(j - 1).wait_send())
+            in_copy(j).start()
+
         pl.when(b == 1)(lambda: out_local(fin, j).start())
         pl.when(b == 0)(lambda: out_remote(fin, j).start())
         return carry
@@ -248,13 +234,12 @@
         for t in (j, half + j):
             pl.when(has_up)(lambda t=t: halo_up(t).wait_send())
             pl.when(has_down)(lambda t=t: halo_down(t).wait_send())
-        for r in range(2):
-            pl.when(jnp.logical_not(last))(lambda r=r: in_copy(j, r).wait_send())
         out_local(mid, j).wait()
         out_remote(mid, j).wait()
         return carry
 
     lax.fori_loop(0, half, drain, 0)
+    pl.when(jnp.logical_not(last))(lambda: in_copy(half - 1).wait_send())
 
 
 def shards(
@@ -288,11 +273,11 @@
             pltpu.VMEM((2, 9 * inner, inner), BF16),
             pltpu.VMEM((2, inner, chans), BF16),
             pltpu.VMEM((2, 8, chans), F32),
-            dma((half,)), dma((4,)), dma((half, 2)), dma((half, 2)), dma((half,)), dma((half,)), dma((half,)),
+            dma((half,)), dma((4,)), dma((half,)), dma((half,)), dma((half,)), dma((half,)), dma((half,)),
             dma((2 * half, 2)), dma((2 * half, 2)), dma((4,)), dma((4,)), dma((3, 3)), dma((3, 3)),
         ],
         compiler_params=pltpu.CompilerParams(
-            collective_id=0, has_side_effects=True, vmem_limit_bytes=56 * 1024 * 1024
+            collective_id=0, has_side_effects=True, vmem_limit_bytes=40 * 1024 * 1024
         ),
     )(
         features.reshape(slides, cells, chans),

time: 185 us -> 188 us (1.016)
  Pallas kernels: 174 us -> 176 us
    unnamed x3 -> x9, local copies, waits for them, and re-layouts: 4.81 us -> 7.55 us
    pallas_call x1, Pallas kernels: 174 us -> 176 us  [shards(): pl.pallas_call(functools.partial(kernel, strips, sections, half, cols, ch...]
where the time goes in v3:
time: 188 us
  Pallas kernels  176 us (94%)
  local copies, waits for them, and re-layouts  8.34 us (4%)
  other arithmetic  2.85 us (2%)
    pallas_call x1, Pallas kernels, shards(): pl.pallas_call(functools.partial(kernel, strips, sections, half, cols, ch...  176 us
    unnamed x9, local copies, waits for them, and re-layouts  7.55 us

profile of v3, /device:TPU:29, one launch (start us, length us, event | category | flops | bytes accessed | tf_op | source)
XLA Modules:
  0.0 187.6 jit_solution(4871298502842049463)
XLA Ops:
  0.0 0.8 fusion
  0.8 0.7 convert_element_type.17
  1.5 0.7 convert_element_type.18
  2.2 0.7 pad_convert_fusion
  2.9 0.2 scatter.19
  3.0 0.1 scatter.20.bias
  3.1 0.1 broadcast_in_dim.6
  3.2 0.1 broadcast_in_dim.7
  3.3 0.3 broadcast_in_dim.16.mask
  3.7 0.0 copy-start
  3.7 2.2 %copy-done = bf16[8,2,128,1024]{3,2,1,0:T(8,128)(2,1)S(1)} copy-done((bf16[8,2,128,1024]{3,2,1,0:T(8,128)(2,1)S(1)}, bf16[8,2,128,1024]{3,2,1,0:T(8,128)(2,1)}, u32[]{:S(2)}) %copy-start) | copy-done | bytes 4194328
  5.9 0.0 copy-start.1
  5.9 1.3 copy-done.1
  7.1 0.0 copy-start.2
  7.1 1.0 copy-done.2
  8.2 0.0 copy-start.3
  8.2 1.0 copy-done.3
  9.2 176.4 %shard_map.82 = bf16[8,256,1024]{2,1,0:T(8,128)(2,1)S(1)} custom-call(bf16[8,256,1024]{2,1,0:T(8,128)(2,1)S(1)} %bitcast.9, f32[8,256,128]{2,1,0:T(8,128)S(1)} %broadcast_in_dim.16.mask, bf16[1024,256]{1,0:T(8,128)(2,1)S(1)} %bitcast.11, bf16[2304,256]{1,0:T(8,128)(2,1)S(1)} %bitcast.10, bf16[256,1024]{1,0:T(8,128)(2,1)S(1)} %bitcast.12, ...), custom_call_target="tpu_custom_call" | custom-call | tf_op jit(solution)/shard_map/pallas_call | solution.py:261
  185.6 2.0 %copy.12 = bf16[1,8,2,128,1024]{4,3,2,1,0:T(8,128)(2,1)} copy(bf16[1,8,2,128,1024]{4,3,2,1,0:T(8,128)(2,1)S(1)} %bitcast.8) | data formatting | bytes 8388608
  (1 shorter events, 0.0 us)
Async XLA Ops:
  3.7 2.2 %copy-start = (bf16[8,2,128,1024]{3,2,1,0:T(8,128)(2,1)S(1)}, bf16[8,2,128,1024]{3,2,1,0:T(8,128)(2,1)}, u32[]{:S(2)}) copy-start(bf16[8,2,128,1024]{3,2,1,0:T(8,128)(2,1)} %param.14) | copy-start | bytes 12582916
  5.9 1.3 copy-start.1
  7.1 1.0 copy-start.2
  8.2 1.0 copy-start.3

commit v4 on v1

--- a/solution.py
+++ b/solution.py
@@ -136,12 +136,16 @@
     def dot(lhs, rhs):
         return jnp.dot(lhs, rhs, preferred_element_type=F32)
 
-    def block(which, j, src, dst):
+    def block(which, j, src, dst, arrived, finished):
         t = which * half + j
-        reduced = dot(src[j], v1[which]) + vb[which, 0:1, 0:inner]
-        stage[t] = jnp.maximum(reduced, 0.0).astype(BF16)
-        pl.when(has_up)(lambda: halo_up(t).start())
-        pl.when(has_down)(lambda: halo_down(t).start())
+        for r in range(2):
+            arrived(r)
+            reduced = dot(src[j, pl.ds(r * cols, cols)], v1[which]) + vb[which, 0:1, 0:inner]
+            stage[t, pl.ds(r * cols, cols)] = jnp.maximum(reduced, 0.0).astype(BF16)
+            if r == 0:
+                pl.when(has_up)(lambda: halo_up(t).start())
+            else:
+                pl.when(has_down)(lambda: halo_down(t).start())
 
         def tap(dy, dx):
             return v2[which, pl.ds((dy * 3 + dx) * inner, inner), :]
@@ -162,14 +166,21 @@
         right = jnp.where(column == cols - 1, 0.0, pltpu.roll(sums[2], 2 * cols - 1, 0))
         total = sums[1] + left + right + vb[which, 1:2, 0:inner]
         spatial = jnp.maximum(total, 0.0).astype(BF16)
-        kept = mask[b * half + j][:, 0:1]
-        for low in range(0, chans, inner):
-            span = pl.ds(low, inner)
-            value = src[j, :, span].astype(F32) + dot(spatial, v3[which, :, span]) + vb[which, 2:3, span]
-            dst[j, :, span] = (jnp.maximum(value, 0.0) * kept).astype(BF16)
-
-    def in_copy(j):
-        return remote(fin.at[j], inbuf.at[j], fwd_sem.at[j], in_sem.at[j], ahead)
+        for r in range(2):
+            part = pl.ds(r * cols, cols)
+            kept = mask[b * half + j, part, 0:1]
+            for low in range(0, chans, inner):
+                span = pl.ds(low, inner)
+                value = dot(spatial[r * cols : (r + 1) * cols], v3[which, :, span])
+                value += src[j, part, span].astype(F32) + vb[which, 2:3, span]
+                dst[j, part, span] = (jnp.maximum(value, 0.0) * kept).astype(BF16)
+            finished(r)
+
+    def in_copy(j, r):
+        part = pl.ds(r * cols, cols)
+        return remote(
+            fin.at[j, part], inbuf.at[j, part], fwd_sem.at[j, r], in_sem.at[j, r], ahead
+        )
 
     def out_local(buffer, j):
         return pltpu.make_async_copy(buffer.at[j], out.at[b * half + j], loc_sem.at[j])
@@ -182,8 +193,17 @@
 
     def one_slide(j, carry):
         pl.when(first)(lambda: feat_copy(j).wait())
-        pl.when(jnp.logical_not(first))(lambda: in_copy(j).wait_recv())
-        block(0, j, inbuf, mid)
+
+        def arrived(r):
+            pl.when(jnp.logical_not(first))(lambda: in_copy(j, r).wait_recv())
+
+        def finished(r):
+            pl.when(jnp.logical_not(last))(lambda: in_copy(j, r).start())
+
+        def nothing(r):
+            pass
+
+        block(0, j, inbuf, mid, arrived, nothing)
         pl.when(b == 0)(lambda: out_local(mid, j).start())
         pl.when(b == 1)(lambda: out_remote(mid, j).start())
 
@@ -192,8 +212,7 @@
             pl.when(b == 0)(wait_other)
             pl.when(b == 1)(wait_own)
 
-        block(1, j, mid, fin)
-        pl.when(jnp.logical_not(last))(lambda: in_copy(j).start())
+        block(1, j, mid, fin, nothing, finished)
         pl.when(b == 1)(lambda: out_local(fin, j).start())
         pl.when(b == 0)(lambda: out_remote(fin, j).start())
         return carry
@@ -207,7 +226,8 @@
         for t in (j, half + j):
             pl.when(has_up)(lambda t=t: halo_up(t).wait_send())
             pl.when(has_down)(lambda t=t: halo_down(t).wait_send())
-        pl.when(jnp.logical_not(last))(lambda: in_copy(j).wait_send())
+        for r in range(2):
+            pl.when(jnp.logical_not(last))(lambda r=r: in_copy(j, r).wait_send())
         out_local(mid, j).wait()
         out_remote(mid, j).wait()
         return carry
@@ -246,11 +266,11 @@
             pltpu.VMEM((2, 9 * inner, inner), BF16),
             pltpu.VMEM((2, inner, chans), BF16),
             pltpu.VMEM((2, 8, chans), F32),
-            dma((half,)), dma((4,)), dma((half,)), dma((half,)), dma((half,)), dma((half,)), dma((half,)),
+            dma((half,)), dma((4,)), dma((half, 2)), dma((half, 2)), dma((half,)), dma((half,)), dma((half,)),
             dma((2 * half, 2)), dma((2 * half, 2)), dma((4,)), dma((4,)), dma((3,)), dma((3,)),
         ],
         compiler_params=pltpu.CompilerParams(
-            collective_id=0, has_side_effects=True, vmem_limit_bytes=40 * 1024 * 1024
+            collective_id=0, has_side_effects=True, vmem_limit_bytes=56 * 1024 * 1024
         ),
     )(
         features.reshape(slides, cells, chans),

time: 158 us -> 152 us (0.962); the launches traced: 158 us -> 150 us
  Pallas kernels: 146 us -> 140 us
  local copies, waits for them, and re-layouts: 8.34 us -> 6.58 us
    pallas_call x1, Pallas kernels: 146 us -> 140 us  [shards(): pl.pallas_call(functools.partial(kernel, strips, sections, half, cols, ch...]
    unnamed x9 -> x3, local copies, waits for them, and re-layouts: 7.55 us -> 4.81 us
where the time goes in v4:
time: 152 us; the launch traced here: 150 us
  Pallas kernels  140 us (92%)
  local copies, waits for them, and re-layouts  6.58 us (4%)
  other arithmetic  2.85 us (2%)
    pallas_call x1, Pallas kernels, shards(): pl.pallas_call(functools.partial(kernel, strips, sections, half, cols, ch...  140 us
    unnamed x3, local copies, waits for them, and re-layouts  4.81 us

profile of v4, /device:TPU:29, one launch (start us, length us, event | category | flops | bytes accessed | tf_op | source)
XLA Modules:
  0.0 149.8 jit_solution(3890526497468277438)
XLA Ops:
  0.0 0.8 fusion
  0.8 0.7 convert_element_type.17
  1.5 0.7 convert_element_type.18
  2.2 0.7 pad_convert_fusion
  2.9 0.2 scatter.19
  3.0 0.1 scatter.20.bias
  3.1 0.0 copy-start
  3.1 0.1 broadcast_in_dim.6
  3.2 0.1 broadcast_in_dim.7
  3.3 1.3 broadcast_in_dim.16.mask
  4.7 0.0 copy-done
  4.7 140.3 %shard_map.82 = bf16[8,256,1024]{2,1,0:T(8,128)(2,1)} custom-call(bf16[8,256,1024]{2,1,0:T(8,128)(2,1)} %bitcast.9, f32[8,256,128]{2,1,0:T(8,128)} %broadcast_in_dim.16.mask, bf16[1024,256]{1,0:T(8,128)(2,1)} %bitcast.11, bf16[2304,256]{1,0:T(8,128)(2,1)} %bitcast.10, bf16[256,1024]{1,0:T(8,128)(2,1)} %bitcast.12, f32[8,1024]{1,0:T(8,128)} %copy-done), custom_call_target="tpu_custom_call" | custom-call | tf_op jit(solution)/shard_map/pallas_call | solution.py:254
  145.0 4.8 %copy.12 = bf16[1,8,2,128,1024]{4,3,2,1,0:T(8,128)(2,1)} copy(bf16[1,8,2,128,1024]{4,3,2,1,0:T(8,128)(2,1)} %bitcast.8) | data formatting | bytes 8388608
  (1 shorter events, 0.0 us)
Async XLA Ops:
  3.1 1.5 %copy-start = (f32[8,1024]{1,0:T(8,128)}, f32[8,1024]{1,0:T(8,128)S(1)}, u32[]{:S(2)}) copy-start(f32[8,1024]{1,0:T(8,128)S(1)} %scatter.20.bias) | copy-start | bytes 98308
